TPU v7x, 32 devices: a whole 2x2x4 slice. The times are simulated.
32 devices in a mesh: slab: 16 (over z, y, core), tm: 2 (over x).
Axes of the slice: x: 2, y: 2, z: 4, core: 2. Of those that a mesh axis runs over, the one named last changes fastest.
Arguments:
- recording: bfloat16 [512, 32768], P('tm', 'slab'), may hold values from -6 to 6
- footprints: bfloat16 [2176, 4096], P(None, 'slab'), may hold values from -0.125 to 0.125
- traces: float32 [512, 4096], P('tm', 'slab'), may hold values from 0 to 2
- live_count: int32 [16], replicated, may hold values from 1 to 256, 3072 in all
Outputs:
- new_traces: float32 [512, 4096], P('tm', 'slab')
- new_footprints: bfloat16 [2176, 4096], P('tm', 'slab')
Inputs may be any that keep to these rules, and one draw needn't show every extreme that they name: Slots 0 .. live_count[s] - 1 of slab s are live; some slab has all 256 live.
All inputs are finite; a program needn't handle non-finite values.
Results may differ from a plain program's by a relative error of at most 0.0034.
Values may be sent and summed in bfloat16 or wider, within the bound.
No kernel may reach another device: no remote copies, remote signals or barrier semaphores. Data moves between devices by JAX's collectives and lax.ppermute only.
A program may use at most 64 MiB of HBM per device.

v0:
```python
import jax
import jax.numpy as jnp
from jax import lax
from jax.sharding import PartitionSpec as P

GROUP = 128
GROUPS_DEV = 2


def passed_along(block, axis, distance):
    devices = range(lax.axis_size(axis))
    route = [(i - distance, i) for i in devices if i - distance in devices]
    return lax.ppermute(block, axis, route)


def with_halo(cells, sides, width):
    for axis, dim in sides:
        count = lax.axis_size(axis)
        ends = count - 1
        head = lax.slice_in_dim(cells, 0, width, axis=dim)
        tail = lax.slice_in_dim(cells, cells.shape[dim] - width, cells.shape[dim], axis=dim)
        cells = jnp.concatenate(
            [
                lax.ppermute(tail, axis, [(i, (i + 1) % count) for i in range(ends)]),
                cells,
                lax.ppermute(head, axis, [((i + 1) % count, i) for i in range(ends)]),
            ],
            axis=dim,
        )
    return cells


def contract_first(left, right):
    return lax.dot_general(
        left, right, (((0,), (0,)), ((), ())), preferred_element_type=jnp.float32
    )


def on_device(recording, footprints, traces, live_count):
    slabs = lax.axis_size("slab")
    slab_index = lax.axis_index("slab")
    neurons = traces.shape[1]
    extended = footprints.shape[0]
    voxels = recording.shape[1]
    rim_rows = extended - voxels
    slots = jnp.arange(neurons, dtype=jnp.int32)
    live_here = jnp.sum(jnp.where(jnp.arange(slabs, dtype=jnp.int32) == slab_index, live_count, 0))
    living = slots < live_here
    row_ids = jnp.arange(extended, dtype=jnp.int32)
    kept_mask = living[None, :] & ((row_ids[:, None] < voxels) | (slab_index < slabs - 1))
    masked_foot = jnp.where(kept_mask, footprints, jnp.zeros_like(footprints))
    start_tr = jnp.where(living[None, :], traces, jnp.zeros_like(traces))
    next_edge, movie_rim = passed_along(
        (masked_foot[:rim_rows], recording[:, :rim_rows]), "slab", -1
    )
    prev_rim = passed_along(masked_foot[voxels:], "slab", 1)
    movie_ext = jnp.concatenate([recording, movie_rim], 1)
    drive = jnp.dot(movie_ext, masked_foot, preferred_element_type=jnp.float32)
    gram_own = contract_first(masked_foot, masked_foot)
    gram_prev = contract_first(masked_foot[:rim_rows], prev_rim)
    gram_next = contract_first(masked_foot[voxels:], next_edge)
    diag_own = jnp.diagonal(gram_own) + 1e-06
    halo_tr = with_halo(start_tr, (("slab", 1),), neurons)
    prev_c = halo_tr[:, :neurons]
    next_c = halo_tr[:, 2 * neurons :]
    outside = jnp.dot(prev_c, gram_prev.T, precision=lax.Precision.HIGHEST) + jnp.dot(
        next_c, gram_next.T, precision=lax.Precision.HIGHEST
    )

    def sweep(group_id, current):
        offset = group_id * GROUP
        columns = lax.dynamic_slice_in_dim(gram_own, offset, GROUP, 1)
        coupled = jnp.dot(
            current, columns, precision=lax.Precision.HIGHEST
        ) + lax.dynamic_slice_in_dim(outside, offset, GROUP, 1)
        before = lax.dynamic_slice_in_dim(current, offset, GROUP, 1)
        driven = lax.dynamic_slice_in_dim(drive, offset, GROUP, 1)
        scaled = lax.dynamic_slice_in_dim(diag_own, offset, GROUP, 0)
        updated = jnp.maximum(before + (driven - coupled) / scaled, 0.0)
        return lax.dynamic_update_slice_in_dim(current, updated, offset, 1)

    new_tr = lax.fori_loop(0, GROUPS_DEV, sweep, start_tr)
    rounded = new_tr.astype(jnp.bfloat16)
    side_tr = with_halo(rounded, (("slab", 1),), neurons)
    frames_all = lax.all_gather(side_tr, "tm", axis=0, tiled=True)
    prev_all = frames_all[:, :neurons]
    own_all = frames_all[:, neurons : 2 * neurons]
    next_all = frames_all[:, 2 * neurons :]
    q_own = contract_first(own_all, own_all)
    q_prev = contract_first(prev_all, own_all)
    q_next = contract_first(next_all, own_all)
    divisor = jnp.maximum(jnp.diagonal(q_own), 1.0)
    share_rows = extended // lax.axis_size("tm")
    first_row = lax.axis_index("tm") * share_rows
    blocks = lax.all_to_all(movie_ext, "tm", split_axis=1, concat_axis=0, tiled=True)
    proj_rows = contract_first(blocks, own_all)
    zero_rows = jnp.zeros((voxels, neurons), jnp.bfloat16)
    prev_full = jnp.concatenate([prev_rim, zero_rows], 0)
    next_full = jnp.concatenate([zero_rows, next_edge], 0)
    foot_share = lax.dynamic_slice_in_dim(masked_foot, first_row, share_rows, 0).astype(jnp.float32)
    prev_share = lax.dynamic_slice_in_dim(prev_full, first_row, share_rows, 0).astype(jnp.float32)
    next_share = lax.dynamic_slice_in_dim(next_full, first_row, share_rows, 0).astype(jnp.float32)
    coupling = jnp.dot(foot_share, q_own, precision=lax.Precision.HIGHEST)
    coupling = coupling + jnp.dot(prev_share, q_prev, precision=lax.Precision.HIGHEST)
    coupling = coupling + jnp.dot(next_share, q_next, precision=lax.Precision.HIGHEST)
    new_foot = jnp.maximum(foot_share + (proj_rows - coupling) / divisor, 0.0).astype(jnp.bfloat16)
    return (new_tr, new_foot)


def solution(mesh):
    placed = (P("tm", "slab"), P(None, "slab"), P("tm", "slab"), P())
    return jax.shard_map(
        on_device,
        mesh=mesh,
        in_specs=placed,
        out_specs=(P("tm", "slab"), P("tm", "slab")),
        check_vma=False,
    )
```

profile of v0, /device:TPU:24, one launch (start us, length us, event | category | flops | bytes accessed | tf_op | source)
XLA Modules:
  0.0 77.2 jit_solution(4601563501691836481)
XLA Ops:
  0.6 1.3 %fusion.26 = s32[]{:T(128)} fusion(s32[16]{0:T(128)} %param.9, s32[]{:T(128)S(6)} %axis_index.23), kind=kLoop, calls=%fused_computation.45 | loop fusion | flops 47 | bytes 72 | tf_op jit(solution)/shard_map/reduce_sum | solution.py:47
  1.9 0.6 iota_compare_fusion.1
  2.6 1.1 %copy.10 = f32[256,256]{0,1:T(8,128)S(1)} copy(f32[256,256]{1,0:T(8,128)} %param.8) | data formatting | bytes 524288 | tf_op args[2]
  3.7 0.1 broadcast_select_fusion
  3.8 0.0 copy-start
  3.8 2.9 %collective-permute-start.3 = (f32[256,256]{0,1:T(8,128)S(1)}, f32[256,256]{0,1:T(8,128)}, u32[]{:S(2)}, u32[]{:S(2)}) collective-permute-start(f32[256,256]{0,1:T(8,128)S(1)} %broadcast_select_fusion), channel_id=1, source_target_pairs={{2,0},{4,2},{6,4},{8,6},{10,8},{12,10},{14,12},{16,14},{18,16},{20... | collective-permute-start | bytes 786440 | tf_op jit(solution)/shard_map/ppermute | solution.py:26
  6.7 1.9 %collective-permute-start.1 = (f32[256,256]{0,1:T(8,128)S(1)}, f32[256,256]{0,1:T(8,128)}, u32[]{:S(2)}, u32[]{:S(2)}) collective-permute-start(f32[256,256]{0,1:T(8,128)S(1)} %broadcast_select_fusion), channel_id=1, source_target_pairs={{0,2},{2,4},{4,6},{6,8},{8,10},{10,12},{12,14},{14,16},{16,18},{18... | collective-permute-start | bytes 786440 | tf_op jit(solution)/shard_map/ppermute | solution.py:24
  8.6 1.5 %copy.12 = bf16[256,2048]{0,1:T(8,128)(2,1)S(1)} copy(bf16[256,2048]{1,0:T(8,128)(2,1)} %param.6) | data formatting | bytes 2097152 | tf_op args[0]
  10.1 0.6 slice.30
  10.7 4.5 %collective-permute-start = (bf16[256,128]{0,1:T(8,128)(2,1)}, bf16[256,128]{0,1:T(8,128)(2,1)}, u32[]{:S(2)}, u32[]{:S(2)}) collective-permute-start(bf16[256,128]{0,1:T(8,128)(2,1)} %slice.30), channel_id=1, source_target_pairs={{2,0},{4,2},{6,4},{8,6},{10,8},{12,10},{14,12},{16,14},{18,16},{20... | collective-permute-start | bytes 196616 | tf_op jit(solution)/shard_map/ppermute | solution.py:13
  15.3 1.2 %and_select_fusion = bf16[2176,256]{1,0:T(8,128)(2,1)S(1)} fusion(bf16[2176,256]{1,0:T(8,128)(2,1)S(1)} %copy-done, pred[256]{0:T(512)(128)(4,1)S(1)} %iota_compare_fusion.1, pred[2176]{0:T(1024)(128)(4,1)S(1)} %fusion.22), kind=kLoop, calls=%fused_computation.19 | loop fusion | flops 1114112 | bytes 2230656 | tf_op jit(solution)/shard_map/jit(_where)/select_n | solution.py:51
  16.5 1.9 %collective-permute-start.2 = (bf16[128,256]{1,0:T(8,128)(2,1)S(1)}, bf16[128,256]{1,0:T(8,128)(2,1)S(1)}, u32[]{:S(2)}, u32[]{:S(2)}) collective-permute-start(bf16[128,256]{1,0:T(8,128)(2,1)S(1)} %get-tuple-element.140), channel_id=1, source_target_pairs={{0,2},{2,4},{4,6},{6,8},{8,10},{10,12},{12,14},{14,16},{16,18},{18... | collective-permute-start | bytes 196616 | tf_op jit(solution)/shard_map/ppermute | solution.py:13
  18.4 4.5 %collective-permute-start.4 = (bf16[128,256]{1,0:T(8,128)(2,1)S(1)}, bf16[128,256]{1,0:T(8,128)(2,1)S(1)}, u32[]{:S(2)}, u32[]{:S(2)}) collective-permute-start(bf16[128,256]{1,0:T(8,128)(2,1)S(1)} %get-tuple-element.141), channel_id=1, source_target_pairs={{2,0},{4,2},{6,4},{8,6},{10,8},{12,10},{14,12},{16,14},{18,16},{20... | collective-permute-start | bytes 196616 | tf_op jit(solution)/shard_map/ppermute | solution.py:13
  23.0 0.5 fusion.35
  23.5 2.3 %gather_fusion = f32[256]{0:T(256)S(1)} fusion(f32[256,256]{1,0:T(8,128)S(1)} %fusion.35, s32[256]{0:T(256)S(1)} %bitcast.34), kind=kCustom, calls=%fused_computation | custom fusion | bytes 4096 | tf_op jit(solution)/shard_map/jit(diagonal)/cond/branch_0_fun/gather | solution.py:62
  25.9 1.4 %fusion.33 = f32[256,256]{0,1:T(8,128)S(1)} fusion(bf16[2176,256]{1,0:T(8,128)(2,1)S(1)} %and_select_fusion, bf16[256,128]{0,1:T(8,128)(2,1)} %collective-permute-done, bf16[256,2048]{0,1:T(8,128)(2,1)S(1)} %copy.12), kind=kOutput, calls=%fused_computation.54 | convolution fusion | flops 287440896 | bytes 2490368 | tf_op jit(solution)/shard_map/dot_general | solution.py:58
  27.3 0.2 fusion.29
  27.6 0.0 collective-permute-done.2
  27.6 0.2 fusion.31
  27.8 0.0 collective-permute-done.3
  27.8 1.5 %fusion.36 = f32[256,256]{1,0:T(8,128)S(1)} fusion(f32[256,256]{0,1:T(8,128)} %collective-permute-done.3, f32[256,256]{1,0:T(8,128)S(1)} %fusion.29), kind=kOutput, calls=%fused_computation.57 | convolution fusion | flops 201326592 | bytes 786432 | tf_op jit(solution)/shard_map/dot_general | solution.py:66
  29.4 0.0 collective-permute-done.1
  29.4 1.5 %convolution_add_fusion.2 = f32[256,256]{1,0:T(8,128)S(1)} fusion(f32[256,256]{1,0:T(8,128)S(1)} %fusion.36, f32[256,256]{0,1:T(8,128)} %collective-permute-done.1, f32[256,256]{1,0:T(8,128)S(1)} %fusion.31), kind=kOutput, calls=%fused_computation.20 | convolution fusion | flops 201392128 | bytes 1048576 | tf_op jit(solution)/shard_map/dot_general | solution.py:66
  30.9 1.3 %while.13 = (s32[]{:T(128)}, f32[256,256]{0,1:T(8,128)S(1)}, f32[256,256]{0,1:T(8,128)S(1)}, f32[256,256]{1,0:T(8,128)S(1)}, f32[256,256]{1,0:T(8,128)S(1)}, /*i...) while((s32[]{:T(128)}, f32[256,256]{0,1:T(8,128)S(1)}, f32[256,256]{0,1:T(8,128)S(1)}, ...), condition=%wide.region_2.3_spmd, body=%wide.region_1.2_spmd.sunk | while | flops 100827144 | bytes 1706655 | solution.py:82
  31.0 0.1 dynamic_slice.68
  31.0 0.1 copy.20
  31.1 0.4 fusion.56
  31.6 0.1 dynamic_slice.68
  31.7 0.1 copy.20
  31.8 0.4 fusion.56
  32.3 2.1 %collective-permute-start.6 = (bf16[256,256]{0,1:T(8,128)(2,1)S(1)}, bf16[256,256]{0,1:T(8,128)(2,1)S(1)}, u32[]{:S(2)}, u32[]{:S(2)}) collective-permute-start(bf16[256,256]{0,1:T(8,128)(2,1)S(1)} %convert_element_type.12), channel_id=1, source_target_pairs={{2,0},{4,2},{6,4},{8,6},{10,8},{12,10},{14,12},{16,14},{18,16},{20... | collective-permute-start | bytes 393224 | tf_op jit(solution)/shard_map/ppermute | solution.py:26
  34.4 2.2 %collective-permute-start.5 = (bf16[256,256]{0,1:T(8,128)(2,1)S(1)}, bf16[256,256]{0,1:T(8,128)(2,1)S(1)}, u32[]{:S(2)}, u32[]{:S(2)}) collective-permute-start(bf16[256,256]{0,1:T(8,128)(2,1)S(1)} %convert_element_type.12), channel_id=1, source_target_pairs={{0,2},{2,4},{4,6},{6,8},{8,10},{10,12},{12,14},{14,16},{16,18},{18... | collective-permute-start | bytes 393224 | tf_op jit(solution)/shard_map/ppermute | solution.py:24
  36.6 1.9 %pad_maximum_fusion = bf16[256,2176]{0,1:T(8,128)(2,1)} fusion(bf16[256,128]{0,1:T(8,128)(2,1)} %collective-permute-done, bf16[256,2048]{0,1:T(8,128)(2,1)S(1)} %copy.12), kind=kLoop, calls=%fused_computation.21 | loop fusion | flops 2228224 | bytes 2228224 | tf_op jit(solution)/shard_map/concatenate | solution.py:57
  38.5 3.6 %all-to-all-start = ((bf16[256,2,1088]{0,2,1:T(8,128)(2,1)}), bf16[256,2,1088]{0,2,1:T(8,128)(2,1)S(1)}, u32[]{:S(2)}, u32[]{:S(2)}) async-start(bf16[256,2,1088]{0,2,1:T(8,128)(2,1)} %bitcast.37), calls=%async_computation | async-start | bytes 2228224 | tf_op jit(solution)/shard_map/all_to_all | solution.py:95
  42.1 0.8 %copy.16 = f32[256,256]{1,0:T(8,128)} copy(f32[256,256]{0,1:T(8,128)S(1)} %get-tuple-element.126) | data formatting | bytes 524288
  43.0 22.3 %all_gather.3 = bf16[512,768]{0,1:T(8,128)(2,1)S(1)} all-gather(bf16[256,768]{0,1:T(8,128)(2,1)S(1)} %pad_maximum_fusion.1), channel_id=1, replica_groups=mesh['slab'=16,'tm'=2] {'tm'}, dimensions={0}, use_global_device_ids=true | all-gather | bytes 1179648 | tf_op jit(solution)/shard_map/all_gather | solution.py:85
  65.3 0.3 fusion.19
  65.6 0.3 fusion.13
  65.8 1.0 %fusion.15 = f32[256,256]{1,0:T(8,128)} fusion(bf16[512,768]{0,1:T(8,128)(2,1)S(1)} %all_gather.3), kind=kOutput, calls=%fused_computation.29 | convolution fusion | flops 67108864 | bytes 786432 | tf_op jit(solution)/shard_map/dot_general | solution.py:34
  66.8 2.3 %gather_fusion.1 = f32[256]{0:T(256)S(1)} fusion(f32[256,256]{1,0:T(8,128)S(1)} %fusion.19, s32[256]{0:T(256)S(1)} %bitcast.35), kind=kCustom, calls=%fused_computation.1 | custom fusion | bytes 4096 | tf_op jit(solution)/shard_map/jit(diagonal)/cond/branch_0_fun/gather | solution.py:92
  69.2 0.0 copy-start.1
  69.2 0.6 fusion.11
  69.8 0.3 copy-done.1
  70.1 0.6 convolution_add_fusion.1
  70.8 0.2 copy-done.5
  71.0 1.9 %convolution_add_fusion = f32[1088,256]{1,0:T(8,128)} fusion(f32[1088,256]{1,0:T(8,128)S(1)} %convolution_add_fusion.1, f32[256,256]{1,0:T(8,128)S(1)} %fusion.13, s32[]{:T(128)S(6)} %select_n.38, bf16[128,256]{1,0:T(8,128)(2,1)S(1)} %copy-done.5), kind=kOutput, calls=%fused_computation.12 | convolution fusion | flops 855916544 | bytes 2555908 | tf_op jit(solution)/shard_map/dot_general | solution.py:105
  72.9 1.4 %copy.15 = bf16[2,256,1088]{2,1,0:T(8,128)(2,1)} copy(bf16[2,256,1088]{1,2,0:T(8,128)(2,1)S(1)} %bitcast.36) | data formatting | bytes 2228224 | tf_op jit(solution)/shard_map/all_to_all | solution.py:95
  74.3 2.9 %fusion.10 = bf16[1088,256]{1,0:T(8,128)(2,1)} fusion(f32[1088,256]{1,0:T(8,128)} %convolution_add_fusion, bf16[512,1088]{1,0:T(8,128)(2,1)} %bitcast.38, f32[256]{0:T(256)S(1)} %broadcast_maximum_fusion, bf16[2176,256]{1,0:T(8,128)(2,1)S(1)} %and_select_fusion, s32[]{:T(128)S(6)} %select_n.38, bf16[512,768]{0,1:T(8,128)(2,1)S(1)} %all_gather.3), kind=kOutput, calls=%fused_computation.18 | convolution fusion | flops 286883840 | bytes 3605508 | tf_op jit(solution)/shard_map/dot_general | solution.py:34
  (24 shorter events, 0.2 us)
Async XLA Ops:
  3.8 11.5 %copy-start = (bf16[2176,256]{1,0:T(8,128)(2,1)S(1)}, bf16[2176,256]{1,0:T(8,128)(2,1)}, u32[]{:S(2)}) copy-start(bf16[2176,256]{1,0:T(8,128)(2,1)} %param.7) | copy-start | bytes 3342340
  3.8 24.0 %collective-permute-start.3 = (f32[256,256]{0,1:T(8,128)S(1)}, f32[256,256]{0,1:T(8,128)}, u32[]{:S(2)}, u32[]{:S(2)}) collective-permute-start(f32[256,256]{0,1:T(8,128)S(1)} %broadcast_select_fusion), channel_id=1, source_target_pairs={{2,0},{4,2},{6,4},{8,6},{10,8},{12,10},{14,12},{16,14},{18,16},{20... | collective-permute-start | bytes 786440 | tf_op jit(solution)/shard_map/ppermute | solution.py:26
  6.7 22.7 %collective-permute-start.1 = (f32[256,256]{0,1:T(8,128)S(1)}, f32[256,256]{0,1:T(8,128)}, u32[]{:S(2)}, u32[]{:S(2)}) collective-permute-start(f32[256,256]{0,1:T(8,128)S(1)} %broadcast_select_fusion), channel_id=1, source_target_pairs={{0,2},{2,4},{4,6},{6,8},{8,10},{10,12},{12,14},{14,16},{16,18},{18... | collective-permute-start | bytes 786440 | tf_op jit(solution)/shard_map/ppermute | solution.py:24
  10.7 15.2 %collective-permute-start = (bf16[256,128]{0,1:T(8,128)(2,1)}, bf16[256,128]{0,1:T(8,128)(2,1)}, u32[]{:S(2)}, u32[]{:S(2)}) collective-permute-start(bf16[256,128]{0,1:T(8,128)(2,1)} %slice.30), channel_id=1, source_target_pairs={{2,0},{4,2},{6,4},{8,6},{10,8},{12,10},{14,12},{16,14},{18,16},{20... | collective-permute-start | bytes 196616 | tf_op jit(solution)/shard_map/ppermute | solution.py:13
  16.5 11.0 %collective-permute-start.2 = (bf16[128,256]{1,0:T(8,128)(2,1)S(1)}, bf16[128,256]{1,0:T(8,128)(2,1)S(1)}, u32[]{:S(2)}, u32[]{:S(2)}) collective-permute-start(bf16[128,256]{1,0:T(8,128)(2,1)S(1)} %get-tuple-element.140), channel_id=1, source_target_pairs={{0,2},{2,4},{4,6},{6,8},{8,10},{10,12},{12,14},{14,16},{16,18},{18... | collective-permute-start | bytes 196616 | tf_op jit(solution)/shard_map/ppermute | solution.py:13
  18.4 8.9 %collective-permute-start.4 = (bf16[128,256]{1,0:T(8,128)(2,1)S(1)}, bf16[128,256]{1,0:T(8,128)(2,1)S(1)}, u32[]{:S(2)}, u32[]{:S(2)}) collective-permute-start(bf16[128,256]{1,0:T(8,128)(2,1)S(1)} %get-tuple-element.141), channel_id=1, source_target_pairs={{2,0},{4,2},{6,4},{8,6},{10,8},{12,10},{14,12},{16,14},{18,16},{20... | collective-permute-start | bytes 196616 | tf_op jit(solution)/shard_map/ppermute | solution.py:13
  27.3 2.0 %copy-start.4 = (bf16[128,256]{1,0:T(8,128)(2,1)}, bf16[128,256]{1,0:T(8,128)(2,1)S(1)}, u32[]{:S(2)}) copy-start(bf16[128,256]{1,0:T(8,128)(2,1)S(1)} %collective-permute-done.4) | copy-start | bytes 196612
  27.6 1.8 %copy-start.2 = (bf16[128,256]{1,0:T(8,128)(2,1)}, bf16[128,256]{1,0:T(8,128)(2,1)S(1)}, u32[]{:S(2)}) copy-start(bf16[128,256]{1,0:T(8,128)(2,1)S(1)} %collective-permute-done.2) | copy-start | bytes 196612
  32.3 10.7 %collective-permute-start.6 = (bf16[256,256]{0,1:T(8,128)(2,1)S(1)}, bf16[256,256]{0,1:T(8,128)(2,1)S(1)}, u32[]{:S(2)}, u32[]{:S(2)}) collective-permute-start(bf16[256,256]{0,1:T(8,128)(2,1)S(1)} %convert_element_type.12), channel_id=1, source_target_pairs={{2,0},{4,2},{6,4},{8,6},{10,8},{12,10},{14,12},{16,14},{18,16},{20... | collective-permute-start | bytes 393224 | tf_op jit(solution)/shard_map/ppermute | solution.py:26
  34.4 8.6 %collective-permute-start.5 = (bf16[256,256]{0,1:T(8,128)(2,1)S(1)}, bf16[256,256]{0,1:T(8,128)(2,1)S(1)}, u32[]{:S(2)}, u32[]{:S(2)}) collective-permute-start(bf16[256,256]{0,1:T(8,128)(2,1)S(1)} %convert_element_type.12), channel_id=1, source_target_pairs={{0,2},{2,4},{4,6},{6,8},{8,10},{10,12},{12,14},{14,16},{16,18},{18... | collective-permute-start | bytes 393224 | tf_op jit(solution)/shard_map/ppermute | solution.py:24
  38.5 34.3 %all-to-all-start = ((bf16[256,2,1088]{0,2,1:T(8,128)(2,1)}), bf16[256,2,1088]{0,2,1:T(8,128)(2,1)S(1)}, u32[]{:S(2)}, u32[]{:S(2)}) async-start(bf16[256,2,1088]{0,2,1:T(8,128)(2,1)} %bitcast.37), calls=%async_computation | async-start | bytes 2228224 | tf_op jit(solution)/shard_map/all_to_all | solution.py:95
  69.2 1.0 %copy-start.1 = (f32[256,256]{1,0:T(8,128)S(1)}, f32[256,256]{1,0:T(8,128)}, u32[]{:S(2)}) copy-start(f32[256,256]{1,0:T(8,128)} %fusion.15) | copy-start | bytes 786436
  69.2 0.9 %copy-start.3 = (bf16[128,256]{1,0:T(8,128)(2,1)S(1)}, bf16[128,256]{1,0:T(8,128)(2,1)}, u32[]{:S(2)}) copy-start(bf16[128,256]{1,0:T(8,128)(2,1)} %copy-done.2) | copy-start | bytes 196612
  70.1 0.8 %copy-start.5 = (bf16[128,256]{1,0:T(8,128)(2,1)S(1)}, bf16[128,256]{1,0:T(8,128)(2,1)}, u32[]{:S(2)}) copy-start(bf16[128,256]{1,0:T(8,128)(2,1)} %copy-done.4) | copy-start | bytes 196612
where the time goes:
time: 77.9 us; the launch traced here: 77.2 us
  starting transfers between devices  23.7 us (30%)
  blocking collectives  22.3 us (29%)
  matrix products  13.8 us (18%)
  local copies, waits for them, and re-layouts  11 us (14%)
  other arithmetic  5.21 us (7%)
  between operations  1 us (1%)
    all_gather x1, blocking collectives, on_device(): frames_all = lax.all_gather(side_tr, 'tm', axis=0, tiled=True)  22.3 us
    ppermute x3, starting transfers between devices, passed_along(): return lax.ppermute(block, axis, route)  11 us
    dot_general x7, matrix products, contract_first(): lax.dot_general(left, right, (((0,), (0,)), ((), ())), preferred_element_...  5.33 us
    ppermute x2, starting transfers between devices, with_halo(): lax.ppermute(head, axis, [((i + 1) % count, i) for i in range(ends)])  5.02 us
    ppermute x2, starting transfers between devices, with_halo(): lax.ppermute(tail, axis, [(i, (i + 1) % count) for i in range(ends)])  4.12 us
    unnamed x15, local copies, waits for them, and re-layouts  3.9 us
    all_to_all x1, starting transfers between devices, on_device(): lax.all_to_all(movie_ext, 'tm', split_axis=1, concat_axis=0, tiled=True)  3.59 us
    gather x1, local copies, waits for them, and re-layouts, on_device(): diag_own = jnp.diagonal(gram_own) + 1e-06  2.34 us
  transfers between devices with their start and end apart: 8, of which 0 were waited for; matrix products, arithmetic and copies ran while one was open for 25% of the time, Pallas kernels for 0%

commit v1 on v0

v1 whole, which is shorter than its diff:
```python
import functools

import jax
import jax.numpy as jnp
from jax import lax
from jax.experimental import pallas as pl
from jax.experimental.pallas import tpu as pltpu
from jax.sharding import PartitionSpec as P

GROUP = 128
BF = jnp.bfloat16
F32 = jnp.float32
WHOLE = pl.BlockSpec(memory_space=pltpu.VMEM)
SCALARS = pl.BlockSpec(memory_space=pltpu.SMEM)
LEFT_THERE = pl.BlockSpec(memory_space=pl.ANY)


def mm(left, right):
    return jnp.dot(left, right, preferred_element_type=F32)


def mm_t(left, right):
    return lax.dot_general(left, right, (((1,), (1,)), ((), ())), preferred_element_type=F32)


def t_mm(left, right):
    return lax.dot_general(left, right, (((0,), (0,)), ((), ())), preferred_element_type=F32)


def halves(wide):
    high = wide.astype(BF)
    return high, (wide - high.astype(F32)).astype(BF)


def living(live_ref, block):
    slots = lax.broadcasted_iota(jnp.int32, block.shape, 1)
    return jnp.where(slots < live_ref[lax.axis_index("slab")], block, jnp.zeros_like(block))


def diagonal(square):
    rows = lax.broadcasted_iota(jnp.int32, square.shape, 0)
    columns = lax.broadcasted_iota(jnp.int32, square.shape, 1)
    return jnp.sum(jnp.where(rows == columns, square, 0.0), axis=0, keepdims=True)


def call(body, outs, in_specs, out_specs, flops, **more):
    return pl.pallas_call(
        body,
        out_shape=outs,
        in_specs=in_specs,
        out_specs=out_specs,
        compiler_params=pltpu.CompilerParams(vmem_limit_bytes=48 * 1024 * 1024),
        cost_estimate=pl.CostEstimate(flops=flops, bytes_accessed=2 ** 21, transcendentals=0),
        **more,
    )


def copied(source, target, sem):
    copy = pltpu.make_async_copy(source, target, sem)
    copy.start()
    return copy


def rim_kernel(voxels, share, live, movie, foot, start, near, far, outgoing, head, tail, sems):
    rim = head.shape[0]
    odd = lax.axis_index("slab") % 2 == 1
    last = lax.axis_index("slab") == lax.axis_size("slab") - 1
    first = copied(foot.at[pl.ds(0, rim)], head, sems.at[0])
    second = copied(foot.at[pl.ds(voxels, rim)], tail, sems.at[1])
    if outgoing is not None:
        take_share(1 - lax.axis_index("tm"), voxels, share, rim, movie, outgoing)
    high, low = halves(living(live, start[...]))
    first.wait()
    second.wait()
    ends = jnp.where(last, jnp.zeros_like(tail[...]), tail[...])
    forward = mm_t(high, ends) + mm_t(low, ends)
    backward = movie[:, :rim].astype(F32) - (mm_t(high, head[...]) + mm_t(low, head[...]))
    near[...] = jnp.where(odd, backward, forward)
    far[...] = jnp.where(odd, forward, backward)


def take_share(which, voxels, share, rim, movie, block):
    @pl.when(which == 0)
    def _():
        block[...] = movie[:, :share]

    @pl.when(which == 1)
    def _():
        block[:, :rim] = movie[:, :rim]
        block[:, rim:] = movie[:, share:]


def drive_kernel(voxels, share, live, movie, foot, drive, gram, kept, masked):
    rim = foot.shape[0] - voxels
    last = lax.axis_index("slab") == lax.axis_size("slab") - 1
    masked[:voxels] = living(live, foot[:voxels])
    ends = living(live, foot[voxels:])
    masked[voxels:] = jnp.where(last, jnp.zeros_like(ends), ends)
    drive[...] = mm(movie[...], masked[:voxels])
    gram[...] = t_mm(masked[...], masked[...])
    if kept is not None:
        take_share(lax.axis_index("tm"), voxels, share, rim, movie, kept)


def sweep_kernel(voxels, live, drive, gram, foot, start, near, far, traces, rounded, head, tail, sems):
    rim = head.shape[0]
    odd = lax.axis_index("slab") % 2 == 1
    last = lax.axis_index("slab") == lax.axis_size("slab") - 1
    first = copied(foot.at[pl.ds(0, rim)], head, sems.at[0])
    second = copied(foot.at[pl.ds(voxels, rim)], tail, sems.at[1])
    square = gram[...]
    scale = diagonal(square) + 1e-06
    square_high, square_low = halves(square)
    current = living(live, start[...])
    one, two = near[...], far[...]
    from_prev = halves(jnp.where(odd, one, two))
    from_next = halves(jnp.where(odd, two, one))
    first.wait()
    second.wait()
    begins = living(live, head[...])
    ends = living(live, tail[...])
    ends = jnp.where(last, jnp.zeros_like(ends), ends)
    pull = drive[...] - (mm(from_prev[0], begins) + mm(from_prev[1], begins))
    pull = pull + (mm(from_next[0], ends) + mm(from_next[1], ends))
    for offset in range(0, current.shape[1], GROUP):
        columns = slice(offset, offset + GROUP)
        high, low = halves(current)
        coupled = mm(high, square_high[:, columns])
        coupled = coupled + mm(high, square_low[:, columns]) + mm(low, square_high[:, columns])
        step = (pull[:, columns] - coupled) / scale[:, columns]
        updated = jnp.maximum(current[:, columns] + step, 0.0)
        parts = [current[:, :offset], updated, current[:, offset + GROUP:]]
        current = jnp.concatenate([part for part in parts if part.shape[1]], axis=1)
    traces[...] = current
    rounded[...] = current.astype(BF)


def edge_kernel(voxels, pairs, *refs):
    foot, refs = refs[0], refs[1:]
    movies, fits = refs[:pairs], refs[pairs:2 * pairs]
    sent, edge, sem = refs[2 * pairs:]
    rim = edge.shape[0]
    ending = lax.axis_index("tm") == 0
    row = pl.multiple_of(jnp.where(ending, voxels, 0), rim)
    copied(foot.at[pl.ds(row, rim)], edge, sem).wait()
    at = 0
    for movie, fit in zip(movies, fits):
        frames = fit.shape[0]
        seen = jnp.where(ending, 0.0, movie[...].astype(F32))
        sent[at:at + frames] = seen - mm_t(fit[...], edge[...])
        at += frames


def places(share, rim):
    closing = lax.axis_index("tm") == lax.axis_size("tm") - 1
    inner = pl.multiple_of(jnp.where(closing, 0, rim), 16)
    outer = pl.multiple_of(jnp.where(closing, share - rim, 0), 16)
    return closing, inner, outer


def inner_kernel(rim, pairs, live, foot, *refs):
    movies, fits = refs[:pairs], refs[pairs:2 * pairs]
    out, quad, part, sem = refs[2 * pairs:]
    share = out.shape[0]
    _, inner, _ = places(share, rim)
    row = pl.multiple_of(lax.axis_index("tm") * share + inner, 16)
    copy = copied(foot.at[pl.ds(row, share - rim)], part, sem)
    square = sum(t_mm(fit[...], fit[...]) for fit in fits)
    quad[...] = square
    scale = jnp.maximum(diagonal(square), 1.0)
    high, low = halves(square)
    total = sum(t_mm(movie[:, rim:], fit[...]) for movie, fit in zip(movies, fits))
    copy.wait()
    own = living(live, part[...])
    total = total - (mm(own, high) + mm(own, low))
    moved = jnp.maximum(own.astype(F32) + total / scale, 0.0)
    out[pl.ds(inner, share - rim)] = moved.astype(BF)


def outer_kernel(pairs, live, foot, sofar, quad, came, *refs):
    movies, fits = refs[:pairs], refs[pairs:2 * pairs]
    out, part, moved, sems = refs[2 * pairs:]
    share, rim = out.shape[0], part.shape[0]
    closing, _, outer = places(share, rim)
    last = lax.axis_index("slab") == lax.axis_size("slab") - 1
    row = pl.multiple_of(lax.axis_index("tm") * share + outer, 16)
    copy = copied(foot.at[pl.ds(row, rim)], part, sems.at[0])
    square = quad[...]
    scale = jnp.maximum(diagonal(square), 1.0)
    high, low = halves(square)
    total = 0.0
    at = 0
    for movie, fit in zip(movies, fits):
        frames = fit.shape[0]
        seen = jnp.where(closing, 0.0, movie[...].astype(F32)) + came[at:at + frames]
        seen_high, seen_low = halves(seen)
        total = total + (t_mm(seen_high, fit[...]) + t_mm(seen_low, fit[...]))
        at += frames
    copy.wait()
    own = living(live, part[...])
    own = jnp.where(closing & last, jnp.zeros_like(own), own)
    total = total - (mm(own, high) + mm(own, low))
    moved[...] = jnp.maximum(own.astype(F32) + total / scale, 0.0).astype(BF)
    copied(moved, out.at[pl.ds(outer, rim)], sems.at[1]).wait()


def on_device(recording, footprints, traces, live_count):
    slabs, parts = lax.axis_size("slab"), lax.axis_size("tm")
    frames, voxels = recording.shape
    extended, neurons = footprints.shape
    rim = extended - voxels
    share = extended // parts
    swaps = parts == 2
    shape = jax.ShapeDtypeStruct
    copies = pltpu.SemaphoreType.DMA
    share_shape = [shape((frames, share), BF)] if swaps else []

    def rims(live, movie, foot, start, near, far, *rest):
        outgoing = rest[0] if swaps else None
        rim_kernel(voxels, share, live, movie, foot, start, near, far, outgoing, *rest[-3:])

    rim_shape = shape((frames, rim), F32)
    near, far, *outgoing = call(
        rims,
        [rim_shape, rim_shape] + share_shape,
        [SCALARS, WHOLE, LEFT_THERE, WHOLE],
        [WHOLE] * (2 + len(share_shape)),
        2 * frames * neurons * rim * 4,
        scratch_shapes=[pltpu.VMEM((rim, neurons), BF)] * 2 + [copies((2,))],
    )(live_count, recording, footprints, traces)

    if swaps:
        other_movie = lax.ppermute(outgoing[0], "tm", [(0, 1), (1, 0)])
    far = lax.ppermute(
        far, "slab", [pair for i in range(1, slabs - 1, 2) for pair in ((i, i + 1), (i + 1, i))]
    )
    near = lax.ppermute(
        near, "slab", [pair for i in range(0, slabs, 2) for pair in ((i, i + 1), (i + 1, i))]
    )

    def drives(live, movie, foot, drive, gram, *rest):
        kept = rest[0] if swaps else None
        drive_kernel(voxels, share, live, movie, foot, drive, gram, kept, rest[-1])

    drive, gram, *kept = call(
        drives,
        [shape((frames, neurons), F32), shape((neurons, neurons), F32)] + share_shape,
        [SCALARS, WHOLE, WHOLE],
        [WHOLE] * (2 + len(share_shape)),
        2 * (frames + neurons) * neurons * extended,
        scratch_shapes=[pltpu.VMEM((extended, neurons), BF)],
    )(live_count, recording, footprints)

    new_tr, rounded = call(
        functools.partial(sweep_kernel, voxels),
        [shape((frames, neurons), F32), shape((frames, neurons), BF)],
        [SCALARS, WHOLE, WHOLE, LEFT_THERE, WHOLE, WHOLE, WHOLE],
        [WHOLE, WHOLE],
        2 * frames * neurons * neurons * 5,
        scratch_shapes=[pltpu.VMEM((rim, neurons), BF)] * 2 + [copies((2,))],
    )(live_count, drive, gram, footprints, traces, near, far)

    if swaps:
        movies = [kept[0], other_movie]
        fits = [rounded, lax.ppermute(rounded, "tm", [(0, 1), (1, 0)])]
    else:
        cut = (parts - 1) * share
        spread = jnp.concatenate([recording[:, :cut], recording[:, :rim], recording[:, cut:]], 1)
        movies = [lax.all_to_all(spread, "tm", split_axis=1, concat_axis=0, tiled=True)]
        fits = [lax.all_gather(rounded, "tm", axis=0, tiled=True)]
    pairs = len(fits)
    lead_specs = [
        pl.BlockSpec((movie.shape[0], rim), lambda i: (0, 0)) for movie in movies
    ]
    total = frames * parts

    sent = call(
        functools.partial(edge_kernel, voxels, pairs),
        shape((total, rim), F32),
        [LEFT_THERE] + lead_specs + [WHOLE] * pairs,
        WHOLE,
        2 * total * neurons * rim,
        grid=(1,),
        scratch_shapes=[pltpu.VMEM((rim, neurons), BF), copies],
    )(footprints, *movies, *fits)
    ahead = [(i * parts, (i + 1) * parts) for i in range(slabs - 1)]
    behind = [((i + 1) * parts - 1 + parts, (i + 1) * parts - 1) for i in range(slabs - 1)]
    came = lax.ppermute(sent, ("slab", "tm"), ahead + behind)

    sofar, quad = call(
        functools.partial(inner_kernel, rim, pairs),
        [shape((share, neurons), BF), shape((neurons, neurons), F32)],
        [SCALARS, LEFT_THERE] + [WHOLE] * (2 * pairs),
        [WHOLE, WHOLE],
        2 * total * neurons * (share + neurons) + 4 * share * neurons * neurons,
        scratch_shapes=[pltpu.VMEM((share - rim, neurons), BF), copies],
    )(live_count, footprints, *movies, *fits)

    new_foot = call(
        functools.partial(outer_kernel, pairs),
        shape((share, neurons), BF),
        [SCALARS, LEFT_THERE, LEFT_THERE, WHOLE, WHOLE] + lead_specs + [WHOLE] * pairs,
        LEFT_THERE,
        2 * total * neurons * rim * 2,
        grid=(1,),
        input_output_aliases={2: 0},
        scratch_shapes=[pltpu.VMEM((rim, neurons), BF)] * 2 + [copies((2,))],
    )(live_count, footprints, sofar, quad, came, *movies, *fits)
    return new_tr, new_foot


def solution(mesh):
    placed = (P("tm", "slab"), P(None, "slab"), P("tm", "slab"), P())
    return jax.shard_map(
        on_device,
        mesh=mesh,
        in_specs=placed,
        out_specs=(P("tm", "slab"), P("tm", "slab")),
        check_vma=False,
    )
```

time: 77.9 us -> 35.9 us (0.46)
  blocking collectives: 22.3 us -> 0 us
  starting transfers between devices: 23.7 us -> 7.57 us
  matrix products: 13.8 us -> 0 us
  Pallas kernels: 0 us -> 10.8 us
  waiting for transfers between devices: 0.02 us -> 9.99 us
  other arithmetic: 5.21 us -> 0 us
  local copies, waits for them, and re-layouts: 11 us -> 6.47 us
    all_gather x1 -> x0, blocking collectives: 22.3 us -> none  [on_device(): frames_all = lax.all_gather(side_tr, 'tm', axis=0, tiled=True)]
    dot_general x15 -> x0, matrix products: 13.8 us -> none  [the longest x7 5.33 us: contract_first(): lax.dot_general(left, right, (((0,), (0,)), ((), ())), preferred_element_...]
    ppermute x7 -> x5, starting transfers between devices: 20.1 us -> 7.57 us  [the longest x1 3.41 us: on_device(): lax.ppermute(far, 'slab', [pair for i in range(1, slabs - 1, 2) for pair...]
    pallas_call x0 -> x6, Pallas kernels: none -> 10.8 us  [the longest x1 3.09 us: on_device(): call(functools.partial(inner_kernel, rim, pairs), [shape((share, neurons)...]
    ppermute x7 -> x5, waiting for transfers between devices: 0.02 us -> 9.99 us  [the longest x1 3.43 us: on_device(): came = lax.ppermute(sent, ('slab', 'tm'), ahead + behind)]
    gather x2 -> x0, local copies, waits for them, and re-layouts: 4.68 us -> none  [the longest x1 2.34 us: on_device(): diag_own = jnp.diagonal(gram_own) + 1e-06]
    all_to_all x1 -> x0, starting transfers between devices: 3.59 us -> none  [on_device(): lax.all_to_all(movie_ext, 'tm', split_axis=1, concat_axis=0, tiled=True)]
    concatenate x3 -> x0, other arithmetic: 1.95 us -> none  [the longest x1 1.91 us: on_device(): movie_ext = jnp.concatenate([recording, movie_rim], 1)]
  transfers between devices with their start and end apart: 8 -> 5, of which waited for: 0 -> 4; matrix products, arithmetic and copies ran while one was open for 25% -> 4% of each run, Pallas kernels for 0% -> 19%
where the time goes in v1:
time: 35.9 us; the launch traced here: 35.6 us
  Pallas kernels  10.8 us (30%)
  waiting for transfers between devices  9.99 us (28%)
  starting transfers between devices  7.57 us (21%)
  local copies, waits for them, and re-layouts  6.47 us (18%)
  between operations  0.75 us (2%)
    unnamed x16, local copies, waits for them, and re-layouts  4.09 us
    ppermute x1, waiting for transfers between devices, on_device(): came = lax.ppermute(sent, ('slab', 'tm'), ahead + behind)  3.43 us
    ppermute x1, starting transfers between devices, on_device(): lax.ppermute(far, 'slab', [pair for i in range(1, slabs - 1, 2) for pair...  3.41 us
    pallas_call x1, Pallas kernels, on_device(): call(functools.partial(inner_kernel, rim, pairs), [shape((share, neurons)...  3.09 us
    ppermute x1, waiting for transfers between devices, on_device(): other_movie = lax.ppermute(outgoing[0], 'tm', [(0, 1), (1, 0)])  3.06 us
    ppermute x1, waiting for transfers between devices, on_device(): lax.ppermute(far, 'slab', [pair for i in range(1, slabs - 1, 2) for pair...  2.47 us
    pallas_call x1, Pallas kernels, on_device(): call(functools.partial(sweep_kernel, voxels), [shape((frames, neurons), F...  2.24 us
    ppermute x1, starting transfers between devices, on_device(): came = lax.ppermute(sent, ('slab', 'tm'), ahead + behind)  2.06 us
  transfers between devices with their start and end apart: 5, of which 4 were waited for; matrix products, arithmetic and copies ran while one was open for 4% of the time, Pallas kernels for 19%

profile of v1, /device:TPU:24, one launch (start us, length us, event | category | flops | bytes accessed | tf_op | source)
XLA Modules:
  0.0 35.6 jit_solution(9748236007118970949)
XLA Ops:
  0.6 0.0 copy-start
  0.6 1.2 %copy-done = bf16[2176,256]{1,0:T(8,128)(2,1)S(1)} copy-done((bf16[2176,256]{1,0:T(8,128)(2,1)S(1)}, bf16[2176,256]{1,0:T(8,128)(2,1)}, u32[]{:S(2)}) %copy-start) | copy-done | bytes 1114136
  1.9 0.0 copy-start.2
  1.9 1.2 %copy-done.2 = bf16[256,2048]{1,0:T(8,128)(2,1)S(1)} copy-done((bf16[256,2048]{1,0:T(8,128)(2,1)S(1)}, bf16[256,2048]{1,0:T(8,128)(2,1)}, u32[]{:S(2)}) %copy-start.2) | copy-done | bytes 1048600
  3.1 0.0 copy-start.4
  3.1 0.9 %copy-done.4 = f32[256,256]{1,0:T(8,128)S(1)} copy-done((f32[256,256]{1,0:T(8,128)S(1)}, f32[256,256]{1,0:T(8,128)}, u32[]{:S(2)}) %copy-start.4) | copy-done | bytes 262168
  4.1 0.0 copy-start.6
  4.1 0.7 %copy-done.6 = s32[16]{0:T(128)S(1)} copy-done((s32[16]{0:T(128)S(1)}, s32[16]{0:T(128)}, u32[]{:S(2)}) %copy-start.6) | copy-done | bytes 88
  4.7 0.0 copy-start.3
  4.7 2.0 %shard_map.60 = (f32[256,128]{1,0:T(8,128)}, f32[256,128]{1,0:T(8,128)S(1)}, bf16[256,1088]{1,0:T(8,128)(2,1)S(1)}) custom-call(s32[16]{0:T(128)S(1)} %copy-done.6, bf16[256,2048]{1,0:T(8,128)(2,1)S(1)} %copy-done.2, bf16[2176,256]{1,0:T(8,128)(2,1)S(1)} %copy-done, f32[256,256]{1,0:T(8,128)S(1)} %copy-done.4), custom_call_target="tpu_custom_call" | custom-call | flops 67108864 | bytes 2097152 | tf_op jit(solution)/shard_map/pallas_call | solution.py:223
  6.7 0.0 copy-start.1
  6.7 0.0 copy-start.7
  6.7 1.0 %copy.7 = bf16[256,1088]{0,1:T(8,128)(2,1)} copy(bf16[256,1088]{1,0:T(8,128)(2,1)S(1)} %get-tuple-element.18) | data formatting | bytes 1114112 | tf_op jit(solution)/shard_map/pallas_call | solution.py:223
  7.7 0.0 copy-start.5
  7.7 1.3 %collective-permute-start.2 = (bf16[256,1088]{0,1:T(8,128)(2,1)}, bf16[256,1088]{0,1:T(8,128)(2,1)}, u32[]{:S(2)}, u32[]{:S(2)}) collective-permute-start(bf16[256,1088]{0,1:T(8,128)(2,1)} %copy.7), channel_id=1, source_target_pairs={{0,1},{1,0},{2,3},{3,2},{4,5},{5,4},{6,7},{7,6},{8,9},{9,8},{10,11... | collective-permute-start | bytes 1671176 | tf_op jit(solution)/shard_map/ppermute | solution.py:233
  9.1 0.0 collective-permute-start
  9.1 3.4 %collective-permute-start.1 = (f32[256,128]{1,0:T(8,128)S(1)}, f32[256,128]{1,0:T(8,128)S(1)}, u32[]{:S(2)}, u32[]{:S(2)}) collective-permute-start(f32[256,128]{1,0:T(8,128)S(1)} %get-tuple-element.15), channel_id=1, source_target_pairs={{2,4},{4,2},{6,8},{8,6},{10,12},{12,10},{14,16},{16,14},{18,20},{2... | collective-permute-start | bytes 393224 | tf_op jit(solution)/shard_map/ppermute | solution.py:234
  12.5 0.0 copy-done.3
  12.5 0.0 copy-done.1
  12.5 0.0 copy-done.7
  12.5 1.3 %shard_map.59 = (f32[256,256]{1,0:T(8,128)S(1)}, f32[256,256]{1,0:T(8,128)S(1)}, bf16[256,1088]{1,0:T(8,128)(2,1)S(1)}) custom-call(s32[16]{0:T(128)S(1)} %copy-done.7, bf16[256,2048]{1,0:T(8,128)(2,1)S(1)} %copy-done.3, bf16[2176,256]{1,0:T(8,128)(2,1)S(1)} %copy-done.1), custom_call_target="tpu_custom_call" | custom-call | flops 570425344 | bytes 2097152 | tf_op jit(solution)/shard_map/pallas_call | solution.py:245
  13.9 0.0 collective-permute-done.near
  13.9 2.5 %collective-permute-done.1.far = f32[256,128]{1,0:T(8,128)S(1)} collective-permute-done((f32[256,128]{1,0:T(8,128)S(1)}, f32[256,128]{1,0:T(8,128)S(1)}, u32[]{:S(2)}, u32[]{:S(2)}) %collective-permute-start.1) | collective-permute-done | bytes 131104 | tf_op jit(solution)/shard_map/ppermute | solution.py:234
  16.4 0.0 copy-done.5
  16.4 2.2 %shard_map.61 = (f32[256,256]{1,0:T(8,128)}, bf16[256,256]{1,0:T(8,128)(2,1)S(1)}) custom-call(s32[16]{0:T(128)S(1)} %copy-done.7, f32[256,256]{1,0:T(8,128)S(1)} %get-tuple-element.12.drive, f32[256,256]{1,0:T(8,128)S(1)} %get-tuple-element.13.gram, bf16[2176,256]{1,0:T(8,128)(2,1)S(1)} %copy-done.1, f32[256,256]{1,0:T(8,128)S(1)} %copy-done.5, ...), custom_call_target="tpu_custom_call" | custom-call | flops 167772160 | bytes 2097152 | tf_op jit(solution)/shard_map/pallas_call | solution.py:254
  18.6 0.8 %collective-permute-start.3 = (bf16[256,256]{1,0:T(8,128)(2,1)S(1)}, bf16[256,256]{1,0:T(8,128)(2,1)S(1)}, u32[]{:S(2)}, u32[]{:S(2)}) collective-permute-start(bf16[256,256]{1,0:T(8,128)(2,1)S(1)} %get-tuple-element.19.refs_2_.refs_3_), channel_id=1, source_target_pairs={{0,1},{1,0},{2,3},{3,2},{4,5},{5,4},{6,7},{7,6},{8,9},{9,8},{10,11... | collective-permute-start | bytes 393224 | tf_op jit(solution)/shard_map/ppermute | solution.py:265
  19.4 3.1 %collective-permute-done.2 = bf16[256,1088]{0,1:T(8,128)(2,1)} collective-permute-done((bf16[256,1088]{0,1:T(8,128)(2,1)}, bf16[256,1088]{0,1:T(8,128)(2,1)}, u32[]{:S(2)}, u32[]{:S(2)}) %collective-permute-start.2) | collective-permute-done | bytes 557088 | tf_op jit(solution)/shard_map/ppermute | solution.py:233
  22.4 1.3 %copy.8.refs_1_.refs_2_ = bf16[256,1088]{1,0:T(8,128)(2,1)S(1)} copy(bf16[256,1088]{0,1:T(8,128)(2,1)} %collective-permute-done.2) | data formatting | bytes 1114112 | tf_op jit(solution)/shard_map/ppermute | solution.py:233
  23.8 1.0 %collective-permute-done.3.refs_3_.refs_4_ = bf16[256,256]{1,0:T(8,128)(2,1)S(1)} collective-permute-done((bf16[256,256]{1,0:T(8,128)(2,1)S(1)}, bf16[256,256]{1,0:T(8,128)(2,1)S(1)}, u32[]{:S(2)}, u32[]{:S(2)}) %collective-permute-start.3) | collective-permute-done | bytes 131104 | tf_op jit(solution)/shard_map/ppermute | solution.py:265
  24.8 0.3 shard_map.63
  25.2 2.1 %collective-permute-start.4 = (f32[512,128]{1,0:T(8,128)S(1)}, f32[512,128]{1,0:T(8,128)S(1)}, u32[]{:S(2)}, u32[]{:S(2)}) collective-permute-start(f32[512,128]{1,0:T(8,128)S(1)} %shard_map.63), channel_id=1, source_target_pairs={{0,2},{2,4},{4,6},{6,8},{8,10},{10,12},{12,14},{14,16},{16,18},{18... | collective-permute-start | bytes 786440 | tf_op jit(solution)/shard_map/ppermute | solution.py:288
  27.2 3.1 %shard_map.62 = (bf16[1088,256]{1,0:T(8,128)(2,1)}, f32[256,256]{1,0:T(8,128)S(1)}) custom-call(s32[16]{0:T(128)S(1)} %copy-done.7, bf16[2176,256]{1,0:T(8,128)(2,1)S(1)} %copy-done.1, bf16[256,1088]{1,0:T(8,128)(2,1)S(1)} %get-tuple-element.17.refs_0_.refs_1_, bf16[256,1088]{1,0:T(8,128)(2,1)S(1)} %copy.8.refs_1_.refs_2_, ...), custom_call_target="tpu_custom_call" | custom-call | flops 637534208 | bytes 2097152 | tf_op jit(solution)/shard_map/pallas_call | solution.py:290
  30.3 3.4 %collective-permute-done.4.came = f32[512,128]{1,0:T(8,128)S(1)} collective-permute-done((f32[512,128]{1,0:T(8,128)S(1)}, f32[512,128]{1,0:T(8,128)S(1)}, u32[]{:S(2)}, u32[]{:S(2)}) %collective-permute-start.4) | collective-permute-done | bytes 262176 | tf_op jit(solution)/shard_map/ppermute | solution.py:288
  33.7 1.8 %shard_map.64 = bf16[1088,256]{1,0:T(8,128)(2,1)} custom-call(s32[16]{0:T(128)S(1)} %copy-done.7, bf16[2176,256]{1,0:T(8,128)(2,1)S(1)} %copy-done.1, bf16[1088,256]{1,0:T(8,128)(2,1)} %get-tuple-element.20.sofar, f32[256,256]{1,0:T(8,128)S(1)} %get-tuple-element.21.quad, ...), custom_call_target="tpu_custom_call", output_to_operand_aliasing={{}: (2, {})} | custom-call | flops 67108864 | bytes 2097152 | tf_op jit(solution)/shard_map/pallas_call | solution.py:299
Async XLA Ops:
  0.6 1.3 %copy-start = (bf16[2176,256]{1,0:T(8,128)(2,1)S(1)}, bf16[2176,256]{1,0:T(8,128)(2,1)}, u32[]{:S(2)}) copy-start(bf16[2176,256]{1,0:T(8,128)(2,1)} %foot.9) | copy-start | bytes 3342340
  1.9 1.2 %copy-start.2 = (bf16[256,2048]{1,0:T(8,128)(2,1)S(1)}, bf16[256,2048]{1,0:T(8,128)(2,1)}, u32[]{:S(2)}) copy-start(bf16[256,2048]{1,0:T(8,128)(2,1)} %movie.3) | copy-start | bytes 3145732
  3.1 0.9 %copy-start.4 = (f32[256,256]{1,0:T(8,128)S(1)}, f32[256,256]{1,0:T(8,128)}, u32[]{:S(2)}) copy-start(f32[256,256]{1,0:T(8,128)} %start.3) | copy-start | bytes 786436
  4.1 0.7 %copy-start.6 = (s32[16]{0:T(128)S(1)}, s32[16]{0:T(128)}, u32[]{:S(2)}) copy-start(s32[16]{0:T(128)} %live.9) | copy-start | bytes 196
  4.7 7.8 %copy-start.3 = (bf16[256,2048]{1,0:T(8,128)(2,1)S(1)}, bf16[256,2048]{1,0:T(8,128)(2,1)}, u32[]{:S(2)}) copy-start(bf16[256,2048]{1,0:T(8,128)(2,1)} %movie.3) | copy-start | bytes 3145732
  6.7 5.8 %copy-start.1 = (bf16[2176,256]{1,0:T(8,128)(2,1)S(1)}, bf16[2176,256]{1,0:T(8,128)(2,1)}, u32[]{:S(2)}) copy-start(bf16[2176,256]{1,0:T(8,128)(2,1)} %foot.9) | copy-start | bytes 3342340
  6.7 5.8 %copy-start.7 = (s32[16]{0:T(128)S(1)}, s32[16]{0:T(128)}, u32[]{:S(2)}) copy-start(s32[16]{0:T(128)} %live.9) | copy-start | bytes 196
  7.7 8.6 %copy-start.5 = (f32[256,256]{1,0:T(8,128)S(1)}, f32[256,256]{1,0:T(8,128)}, u32[]{:S(2)}) copy-start(f32[256,256]{1,0:T(8,128)} %start.3) | copy-start | bytes 786436
  7.7 14.7 %collective-permute-start.2 = (bf16[256,1088]{0,1:T(8,128)(2,1)}, bf16[256,1088]{0,1:T(8,128)(2,1)}, u32[]{:S(2)}, u32[]{:S(2)}) collective-permute-start(bf16[256,1088]{0,1:T(8,128)(2,1)} %copy.7), channel_id=1, source_target_pairs={{0,1},{1,0},{2,3},{3,2},{4,5},{5,4},{6,7},{7,6},{8,9},{9,8},{10,11... | collective-permute-start | bytes 1671176 | tf_op jit(solution)/shard_map/ppermute | solution.py:233
  9.1 4.8 %collective-permute-start = (f32[256,128]{1,0:T(8,128)}, f32[256,128]{1,0:T(8,128)S(1)}, u32[]{:S(2)}, u32[]{:S(2)}) collective-permute-start(f32[256,128]{1,0:T(8,128)} %get-tuple-element.14), channel_id=1, source_target_pairs={{0,2},{2,0},{4,6},{6,4},{8,10},{10,8},{12,14},{14,12},{16,18},{18,... | collective-permute-start | bytes 393224 | tf_op jit(solution)/shard_map/ppermute | solution.py:237
  9.1 7.3 %collective-permute-start.1 = (f32[256,128]{1,0:T(8,128)S(1)}, f32[256,128]{1,0:T(8,128)S(1)}, u32[]{:S(2)}, u32[]{:S(2)}) collective-permute-start(f32[256,128]{1,0:T(8,128)S(1)} %get-tuple-element.15), channel_id=1, source_target_pairs={{2,4},{4,2},{6,8},{8,6},{10,12},{12,10},{14,16},{16,14},{18,20},{2... | collective-permute-start | bytes 393224 | tf_op jit(solution)/shard_map/ppermute | solution.py:234
  18.6 6.2 %collective-permute-start.3 = (bf16[256,256]{1,0:T(8,128)(2,1)S(1)}, bf16[256,256]{1,0:T(8,128)(2,1)S(1)}, u32[]{:S(2)}, u32[]{:S(2)}) collective-permute-start(bf16[256,256]{1,0:T(8,128)(2,1)S(1)} %get-tuple-element.19.refs_2_.refs_3_), channel_id=1, source_target_pairs={{0,1},{1,0},{2,3},{3,2},{4,5},{5,4},{6,7},{7,6},{8,9},{9,8},{10,11... | collective-permute-start | bytes 393224 | tf_op jit(solution)/shard_map/ppermute | solution.py:265
  25.2 8.6 %collective-permute-start.4 = (f32[512,128]{1,0:T(8,128)S(1)}, f32[512,128]{1,0:T(8,128)S(1)}, u32[]{:S(2)}, u32[]{:S(2)}) collective-permute-start(f32[512,128]{1,0:T(8,128)S(1)} %shard_map.63), channel_id=1, source_target_pairs={{0,2},{2,4},{4,6},{6,8},{8,10},{10,12},{12,14},{14,16},{16,18},{18... | collective-permute-start | bytes 786440 | tf_op jit(solution)/shard_map/ppermute | solution.py:288
